TPU v7x, 32 devices: a whole 2x2x4 slice. The times are simulated.
32 devices in a mesh: scen: 2 (over x), row: 16 (over z, y, core).
Axes of the slice: x: 2, y: 2, z: 4, core: 2. Of those that a mesh axis runs over, the one named last changes fastest.
Arguments:
- basin_state: float32 [6, 256, 2048], P('scen', 'row'), parts along dimension 0, may hold values from -1.5 to 1.5
- basin_depth: float32 [256, 4096], P('row', 'scen'), parts along dimension 1, may hold values from 0.7 to 1.5
- coast_depth: float32 [16, 512, 256], P('row', 'scen'), parts along dimension 1, may hold values from 0.1 to 2
- coast_flow: float32 [16, 4, 256, 256], P('row', 'scen'), parts along dimension 1, may hold values from -0.4 to 0.4
- coast_link: int32 [16, 6], P('row', 'scen'), parts along dimension 1, may hold values from 0 to 2031, as said below
Outputs:
- basin_out: float32 [6, 256, 2048], P('scen', 'row'), parts along dimension 0
- coast_out: float32 [16, 6, 256, 256], P('row', 'scen'), parts along dimension 1
There are 2 independent parts, one for each index of `scen`. A program takes and returns all parts, laid end to end along the dimension named above; each array names one. Nothing has to cross between parts.
Inputs may be any that keep to these rules, and one draw needn't show every extreme that they name: `coast_link`: column 0 is a basin row below 256, column 1 a column at most 2031, column 2 is 0 or 1; block 0 links to the last row and last start column, block 1 to row 0 and column 0.
All inputs are finite; a program needn't handle non-finite values.
Results may differ from a plain program's by a relative error of at most 0.0003.
Values sent between devices are 32-bit elements; how exact they have to be, the bound alone decides.
No kernel may reach another device: no remote copies, remote signals or barrier semaphores. Data moves between devices by JAX's collectives and lax.ppermute only.
A program may use at most 64 MiB of HBM per device.

v0:
```python
import functools

import jax
import jax.numpy as jnp
from jax import lax
from jax.experimental import pallas as pl
from jax.experimental.pallas import tpu as pltpu
from jax.sharding import PartitionSpec as P

BSTEPS = 8
CSTEPS = 10

depth_floor = 0.2
ghost_level = 2.0

RATE = 0.05
DEPTH_UNIT = RATE * RATE
FLOW_UNIT = RATE * RATE * RATE
TINY = 1e-30

HALO = BSTEPS
SUB = 8
LANES = 128


def lane_ids():
    return lax.broadcasted_iota(jnp.int32, (SUB, LANES), 1)


def row_ids():
    return lax.broadcasted_iota(jnp.int32, (SUB, LANES), 0)


def cell_terms(u):
    h, mu, mv = u
    r = pl.reciprocal(jnp.maximum(h, depth_floor * DEPTH_UNIT), approx=True)
    vx, vy = mu * r, mv * r
    hp = jnp.maximum(h, TINY)
    c = hp * lax.rsqrt(hp)
    p = (0.5 * h) * h
    cross = mu * vy
    return {
        "u": u,
        "fx": (mu, mu * vx + p, cross),
        "fy": (mv, cross, mv * vy + p),
        "sx": jnp.abs(vx) + c,
        "sy": jnp.abs(vy) + c,
    }


def y_face(above, below):
    a = jnp.maximum(above["sy"], below["sy"])
    return [
        a * (ub - ua) - (fa + fb)
        for ua, ub, fa, fb in zip(above["u"], below["u"], above["fy"], below["fy"])
    ]


def coast_steps(state, terms, after, parts, rows, group, steps, ghost):
    lane, sub = lane_ids(), row_ids()
    first, last = lane == 0, lane == LANES - 1
    top, bottom = sub == 0, sub == SUB - 1
    zero = jnp.zeros((SUB, LANES), jnp.float32)
    left = functools.partial(pltpu.roll, shift=LANES - 1, axis=1)
    right = functools.partial(pltpu.roll, shift=1, axis=1)

    def load(k):
        return [[state[f, half, 1 + k] for f in range(3)] for half in range(2)]

    def store(k, both):
        for half in range(2):
            for f in range(3):
                state[f, half, 1 + k] = both[half][f]

    def wrapped(tail, head):
        down = functools.partial(pltpu.roll, shift=1, axis=0)
        out = {"sy": jnp.where(top, head["sy"], down(tail["sy"]))}
        for name in ("u", "fy"):
            out[name] = [jnp.where(top, h, down(t)) for h, t in zip(head[name], tail[name])]
        return out

    def terms_of(begin, k):
        even, odd = [cell_terms(u) for u in load(begin + k)]
        for half, cell in enumerate((even, odd)):
            for q, value in enumerate((cell["sx"], cell["sy"], cell["fx"][1], cell["fy"][2], cell["fx"][2])):
                terms[half, k, q] = value
        moved = zip(even["u"] + [even["sx"]] + list(even["fx"][1:]), odd["u"] + [odd["sx"]] + list(odd["fx"][1:]))
        for q, (e, o) in enumerate(moved):
            after[k, q] = jnp.where(last, o, left(e))

    def x_faces(begin, k):
        even, odd = load(begin + k)
        following = [after[k, f] for f in range(3)]
        sx_e, sx_o, sx_n = terms[0, k, 0], terms[1, k, 0], after[k, 3]
        fx_e = [even[1], terms[0, k, 2], terms[0, k, 4]]
        fx_o = [odd[1], terms[1, k, 2], terms[1, k, 4]]
        fx_n = [following[1], after[k, 4], after[k, 5]]
        a_in, a_out = jnp.maximum(sx_e, sx_o), jnp.maximum(sx_o, sx_n)
        for f in range(3):
            g_in = a_in * (odd[f] - even[f]) - (fx_e[f] + fx_o[f])
            g_out = a_out * (following[f] - odd[f]) - (fx_o[f] + fx_n[f])
            parts[k, f] = even[f] + g_in
            parts[k, 3 + f] = odd[f] + (g_out - g_in)
            parts[k, 6 + f] = jnp.where(first, -2.0 * fx_e[f], right(g_out))

    def y_cells(begin, k):
        return [
            {"u": u, "fy": [u[2], terms[half, k, 4], terms[half, k, 3]], "sy": terms[half, k, 1]}
            for half, u in enumerate(load(begin + k))
        ]

    def step(_, carry):
        tails, heads = [[cell_terms(u) for u in load(k)] for k in (rows - 1, 0)]
        above = [wrapped(t, g) for t, g in zip(tails, ghost)]
        start = [y_face(a, b) for a, b in zip(above, heads)]

        def rows_from(begin, prev, acc):
            for k in range(group):
                terms_of(begin, k)
            for k in range(group):
                x_faces(begin, k)
            for k in range(group):
                cur = y_cells(begin, k)
                face = [y_face(a, b) for a, b in zip(prev, cur)]
                store(begin + k - 1, [[x + g for x, g in zip(*pair)] for pair in zip(acc, face)])
                acc = [
                    [parts[k, f] - (parts[k, 6 + f] + face[0][f]) for f in range(3)],
                    [parts[k, 3 + f] - face[1][f] for f in range(3)],
                ]
                prev = cur
            return prev, acc

        prev, acc = lax.fori_loop(
            0,
            rows // group,
            lambda i, c: rows_from(i * group, *c),
            (above, [[zero] * 3 for _ in range(2)]),
        )
        end = [
            [
                jnp.where(bottom, -(f + f), pltpu.roll(g, SUB - 1, 0))
                for f, g in zip(cell["fy"], gs)
            ]
            for cell, gs in zip(prev, start)
        ]
        store(rows - 1, [[x + g for x, g in zip(*pair)] for pair in zip(acc, end)])
        return carry

    lax.fori_loop(0, steps, step, 0)


GROUP = 16
UNITS = (DEPTH_UNIT, FLOW_UNIT, FLOW_UNIT)
VMEM_LIMIT = 12 * 1024 * 1024
HALF = LANES // 2


def pick(values, ids):
    return jnp.take_along_axis(values, ids, axis=1, mode="promise_in_bounds")


def split_columns(west, east):
    lane = lane_ids()
    low = lane < HALF
    twice = 2 * jnp.where(low, lane, lane - HALF)
    w = pick(west, jnp.where(low, twice, twice + 1))
    e = pick(east, jnp.where(low, twice + 1, twice))
    return jnp.where(low, w, e), pltpu.roll(jnp.where(low, e, w), HALF, 1)


def join_columns(even, odd):
    lane = lane_ids()
    low = lane < HALF
    odd = pltpu.roll(odd, HALF, 1)
    w, e = jnp.where(low, even, odd), jnp.where(low, odd, even)
    half, is_odd = lane // 2, lane % 2
    return pick(w, half + HALF * is_odd), pick(e, half + HALF * (1 - is_odd))


HALVES = (slice(0, LANES), slice(LANES, 2 * LANES))
TALL = 32


def fold_kernel(depth, flow, state, tmp):
    rows = depth.shape[0] // SUB

    def copy_in(i, carry):
        at = pl.ds(pl.multiple_of(i * TALL, TALL), TALL)
        for f in range(3):
            raw = depth[at] if f == 0 else flow[f - 1, at]
            for p in range(2):
                tmp[f, p, at] = raw[:, HALVES[p]] * UNITS[f]
        return carry

    def fold(k, carry):
        for f in range(3):
            both = split_columns(*[tmp[f, p, pl.ds(k, SUB, stride=rows), :] for p in range(2)])
            for p in range(2):
                state[f, p, k] = both[p]
        return carry

    lax.fori_loop(0, depth.shape[0] // TALL, copy_in, 0)
    lax.fori_loop(0, rows, fold, 0, unroll=4)


def coast_fold(depth, flow):
    cells = depth.shape[0]
    vmem = pl.BlockSpec(memory_space=pltpu.VMEM)
    return pl.pallas_call(
        fold_kernel,
        out_shape=jax.ShapeDtypeStruct((3, 2, cells // SUB, SUB, LANES), jnp.float32),
        in_specs=[vmem, vmem],
        out_specs=vmem,
        scratch_shapes=[pltpu.VMEM((3, 2, cells, LANES), jnp.float32)],
        compiler_params=pltpu.CompilerParams(vmem_limit_bytes=VMEM_LIMIT),
        cost_estimate=pl.CostEstimate(
            flops=CSTEPS * 70 * cells * cells, bytes_accessed=24 * cells * cells, transcendentals=0
        ),
        name="coast_fold",
    )(depth, flow)


def coast_kernel(links, ghosts, folded, depth, flow, out, state, terms, after, parts, tmp):
    rows = depth.shape[0] // SUB
    wet = links[0, 0, 2] > 0

    def copy_dry(i, carry):
        at = pl.ds(pl.multiple_of(i * TALL, TALL), TALL)
        for f in range(3):
            out[f, at] = depth[at] if f == 0 else flow[f - 1, at]
        return carry

    def copy_in(k, carry):
        for f in range(3):
            for p in range(2):
                state[f, p, 1 + k] = folded[f, p, k]
        return carry

    def unfold(k, carry):
        for f in range(3):
            both = join_columns(state[f, 0, 1 + k], state[f, 1, 1 + k])
            for p in range(2):
                tmp[f, p, pl.ds(k, SUB, stride=rows), :] = both[p]
        return carry

    def copy_out(i, carry):
        at = pl.ds(pl.multiple_of(i * TALL, TALL), TALL)
        for f in range(3):
            for p in range(2):
                out[f, at, HALVES[p]] = tmp[f, p, at] * (1.0 / UNITS[f])
        return carry

    @pl.when(jnp.logical_not(wet))
    def _():
        lax.fori_loop(0, depth.shape[0] // TALL, copy_dry, 0)

    @pl.when(wet)
    def _():
        lax.fori_loop(0, rows, copy_in, 0, unroll=4)
        values = jnp.sum(ghosts[...], axis=0)
        level = (ghost_level + values[0:1]) * DEPTH_UNIT
        inflow = values[1:2] * FLOW_UNIT
        spread = [jnp.broadcast_to(v[:, half], (SUB, LANES)) for v in (level, inflow) for half in HALVES]
        h, mv = split_columns(*spread[:2]), split_columns(*spread[2:])
        ghost = [cell_terms([h[p], jnp.zeros_like(h[p]), mv[p]]) for p in range(2)]
        coast_steps(state, terms, after, parts, rows, GROUP, CSTEPS, ghost)
        lax.fori_loop(0, rows, unfold, 0, unroll=4)
        lax.fori_loop(0, depth.shape[0] // TALL, copy_out, 0)


def coast_run(links, ghosts, folded, depth, flow):
    cells = depth.shape[0]
    vmem = pl.BlockSpec(memory_space=pltpu.VMEM)
    return pl.pallas_call(
        coast_kernel,
        out_shape=jax.ShapeDtypeStruct((3, cells, cells), jnp.float32),
        in_specs=[pl.BlockSpec(memory_space=pltpu.SMEM), vmem, vmem, vmem, vmem],
        out_specs=vmem,
        scratch_shapes=[
            pltpu.VMEM((3, 2, 1 + cells // SUB, SUB, LANES), jnp.float32),
            pltpu.VMEM((2, GROUP, 5, SUB, LANES), jnp.float32),
            pltpu.VMEM((GROUP, 6, SUB, LANES), jnp.float32),
            pltpu.VMEM((GROUP, 9, SUB, LANES), jnp.float32),
            pltpu.VMEM((3, 2, cells, LANES), jnp.float32),
        ],
        compiler_params=pltpu.CompilerParams(vmem_limit_bytes=VMEM_LIMIT),
        cost_estimate=pl.CostEstimate(
            flops=CSTEPS * 70 * cells * cells, bytes_accessed=24 * cells * cells, transcendentals=0
        ),
        name="coast_steps",
    )(links, ghosts, folded, depth, flow)


def basin_kernel(state, depth, pair_state, pair_depth, edge, out, eta, hu, hv, dep):
    rows, width = depth.shape
    total = rows + 2 * HALO
    chunks = width // LANES
    position = lax.axis_index("row")
    odd = position % 2
    north_inside = (position < lax.axis_size("row") - 1).astype(jnp.float32)
    pair_from = pl.multiple_of(odd * (rows - HALO), HALO)
    pair_at = pl.multiple_of((1 - odd) * (HALO + rows), HALO)
    edge_at = pl.multiple_of(odd * (HALO + rows), HALO)
    for ref, field, unit in ((eta, 0, 1.0), (hu, 1, 0.5), (hv, 2, 0.5), (dep, 3, 0.25)):
        own, pair = (depth, pair_depth) if field == 3 else (state.at[field], pair_state.at[field])
        ref[HALO : HALO + rows] = own[...] * unit
        ref[pl.ds(pair_at, HALO)] = pair[pl.ds(pair_from, HALO)] * unit
        ref[pl.ds(edge_at, HALO)] = edge[field] * unit
    lane = lax.broadcasted_iota(jnp.int32, (total, LANES), 1)
    first, last = lane == 0, lane == LANES - 1
    row = lax.broadcasted_iota(jnp.int32, (total, LANES), 0)
    kept = jnp.where(row < HALO + rows, 1.0, north_inside)

    def step(_, carry):
        prev_west = jnp.zeros((total, LANES), jnp.float32)
        prev_eta, prev_east, prev_hu = None, None, None
        for c in range(chunks + 1):
            if c < chunks:
                at = slice(c * LANES, (c + 1) * LANES)
                u, v = hu[:, at], hv[:, at]
                west = pltpu.roll(u, 1, 1)
                du = u - jnp.where(first, prev_west, west)
                dv = v - pltpu.roll(v, 1, 0)
                new = (eta[:, at] - (du + dv)) * kept
                eta[:, at] = new
                east = pltpu.roll(new, LANES - 1, 1)
                hv[:, at] = v - dep[:, at] * (pltpu.roll(new, total - 1, 0) - new)
            else:
                east = jnp.zeros((total, LANES), jnp.float32)
            if c > 0:
                back = slice((c - 1) * LANES, c * LANES)
                hu[:, back] = prev_hu - dep[:, back] * (jnp.where(last, east, prev_east) - prev_eta)
            prev_west, prev_eta, prev_east, prev_hu = west, new, east, u
        return carry

    lax.fori_loop(0, BSTEPS, step, 0)
    own = slice(HALO, HALO + rows)
    out[0] = eta[own]
    out[1] = hu[own] * 2.0
    out[2] = hv[own] * 2.0


def basin_run(state, depth, pair_state, pair_depth, edge):
    rows, width = depth.shape
    total = rows + 2 * HALO
    vmem = pl.BlockSpec(memory_space=pltpu.VMEM)
    return pl.pallas_call(
        basin_kernel,
        out_shape=jax.ShapeDtypeStruct((3, rows, width), jnp.float32),
        in_specs=[vmem] * 5,
        out_specs=vmem,
        scratch_shapes=[pltpu.VMEM((total, width), jnp.float32)] * 4,
        compiler_params=pltpu.CompilerParams(vmem_limit_bytes=VMEM_LIMIT),
        cost_estimate=pl.CostEstimate(
            flops=BSTEPS * 16 * total * width, bytes_accessed=4 * 11 * rows * width, transcendentals=0
        ),
        name="basin_steps",
    )(state, depth, pair_state, pair_depth, edge)


def strips_kernel(links, own, pair, ghosts, strips):
    rows, width = own.shape[1], own.shape[2]
    count, cells = ghosts.shape[0], ghosts.shape[2]
    span = 2 * LANES
    position = lax.axis_index("row")
    tops = (position * rows, (position + 1 - 2 * (position % 2)) * rows)

    def piece(b, carry):
        col = links[b, 0, 1]
        start = jnp.clip(col // LANES, 0, width // LANES - 2) * LANES
        shift = lax.rem(span - (col - start), span)
        at = pl.ds(pl.multiple_of(start, LANES), span)
        for i, f in enumerate((0, 2)):
            chunk = None
            for source, top in zip((own, pair), tops):
                row = links[b, 0, 0] - top
                owned = jnp.logical_and(row >= 0, row < rows).astype(jnp.float32)
                part = source[f, pl.ds(jnp.clip(row, 0, rows - 1), 1), at] * owned
                chunk = part if chunk is None else chunk + part
            strips[pl.ds(2 * b + i, 1), :] = pltpu.roll(chunk, shift, 1)[:, :LANES]
        return carry

    lax.fori_loop(0, count, piece, 0, unroll=8)
    at = lax.broadcasted_iota(jnp.int32, (LANES, cells), 0)
    cols = lax.broadcasted_iota(jnp.int32, (LANES, cells), 1)
    base = cols // 16
    weight = ((cols % 16).astype(jnp.float32) + 0.5) / 16.0
    mix = jnp.where(at == base, 1.0 - weight, 0.0) + jnp.where(at == base + 1, weight, 0.0)
    values = jnp.dot(
        strips[...], mix, precision=lax.Precision.HIGHEST, preferred_element_type=jnp.float32
    )
    for b in range(count):
        ghosts[b] = values[2 * b : 2 * b + 2]


def make_strips(links, own, pair, cells):
    count = links.shape[0]
    vmem = pl.BlockSpec(memory_space=pltpu.VMEM)
    smem = pl.BlockSpec(memory_space=pltpu.SMEM)
    return pl.pallas_call(
        strips_kernel,
        out_shape=jax.ShapeDtypeStruct((count, 2, cells), jnp.float32),
        in_specs=[smem, vmem, vmem],
        out_specs=vmem,
        scratch_shapes=[pltpu.VMEM((2 * count, LANES), jnp.float32)],
        compiler_params=pltpu.CompilerParams(vmem_limit_bytes=VMEM_LIMIT),
        name="strips",
    )(links, own, pair)


def local(basin_state, basin_depth, coast_depth, coast_flow, coast_link):
    devices = lax.axis_size("row")
    odd = lax.axis_index("row") % 2
    parity = [list(range(p, devices, 2)) for p in range(2)]
    sent = jnp.broadcast_to(coast_link, (devices // 2,) + coast_link.shape)
    links = lax.all_to_all(sent, "row", 0, 0, axis_index_groups=parity, tiled=True)

    depth, flow = coast_depth[0], coast_flow[0]
    folded = coast_fold(depth, flow)
    basin_state, folded = lax.optimization_barrier((basin_state, folded))

    twins = [(i, i ^ 1) for i in range(devices)]
    pair_state, pair_depth = [lax.ppermute(a, "row", twins) for a in (basin_state, basin_depth)]
    rows = basin_depth.shape[0]
    whole = jnp.concatenate([basin_state, basin_depth[None]], axis=0)
    edge = jnp.where(odd == 1, whole[:, rows - HALO :], whole[:, :HALO])
    across = [(i, i + 1) for i in range(1, devices - 1, 2)]
    edge = lax.ppermute(edge, "row", across + [(j, i) for i, j in across])

    ghosts = make_strips(links, basin_state, pair_state, coast_depth.shape[2])
    edge, ghosts = lax.optimization_barrier((edge, ghosts))
    ghosts = lax.all_to_all(ghosts, "row", 0, 0, axis_index_groups=parity, tiled=True)
    basin_out = basin_run(basin_state, basin_depth, pair_state, pair_depth, edge)
    folded, basin_out = lax.optimization_barrier((folded, basin_out))
    coast_out = coast_run(sent, ghosts, folded, depth, flow)
    return (basin_out, coast_out[None])


def solution(mesh):
    in_specs = (
        P("scen", "row", None),
        P("row", "scen"),
        P("row", "scen", None),
        P("row", "scen", None, None),
        P("row", "scen"),
    )
    out_specs = (P("scen", "row", None), P("row", "scen", None, None))
    return jax.shard_map(local, mesh=mesh, in_specs=in_specs, out_specs=out_specs, check_vma=False)
```

profile of v0, /device:TPU:0, one launch (start us, length us, event | category | flops | bytes accessed | tf_op | source)
XLA Modules:
  0.0 41.6 jit_solution(8692051872221037268)
XLA Ops:
  0.6 0.0 copy-start.1
  0.6 1.0 %copy-done.1 = f32[1,2,256,256]{3,2,1,0:T(8,128)S(1)} copy-done((f32[1,2,256,256]{3,2,1,0:T(8,128)S(1)}, f32[1,2,256,256]{3,2,1,0:T(8,128)}, u32[]{:S(2)}) %copy-start.1) | copy-done | bytes 524312
  1.7 0.0 copy-start.3
  1.7 0.9 %copy-done.3 = f32[1,256,256]{2,1,0:T(8,128)S(1)} copy-done((f32[1,256,256]{2,1,0:T(8,128)S(1)}, f32[1,256,256]{2,1,0:T(8,128)}, u32[]{:S(2)}) %copy-start.3) | copy-done | bytes 262168
  2.6 0.0 copy-start
  2.6 0.0 copy-start.5
  2.6 1.7 %coast_fold.1.folded = f32[3,2,32,8,128]{4,3,2,1,0:T(8,128)S(1)} custom-call(f32[256,256]{1,0:T(8,128)S(1)} %bitcast.7, f32[2,256,256]{2,1,0:T(8,128)S(1)} %bitcast.5), custom_call_target="tpu_custom_call" | custom-call | flops 45875200 | bytes 1572864 | tf_op jit(solution)/shard_map/coast_fold/pallas_call | solution.py:209
  4.3 0.0 copy-done
  4.3 0.5 %collective-permute-start = (f32[3,16,2048]{2,1,0:T(8,128)S(1)}, f32[3,16,2048]{2,1,0:T(8,128)S(1)}, u32[]{:S(2)}, u32[]{:S(2)}) collective-permute-start(f32[3,16,2048]{2,1,0:T(8,128)S(1)} %copy-done), channel_id=1, source_target_pairs={{0,1},{1,0},{2,3},{3,2},{4,5},{5,4},{6,7},{7,6},{8,9},{9,8},{10,11... | collective-permute-start | bytes 1179656 | tf_op jit(solution)/shard_map/ppermute | solution.py:423
  4.8 0.0 copy-done.5
  4.9 0.0 copy-start.6
  4.9 0.7 %collective-permute-start.2 = (f32[4,8,2048]{2,1,0:T(8,128)S(1)}, f32[4,8,2048]{2,1,0:T(8,128)S(1)}, u32[]{:S(2)}, u32[]{:S(2)}) collective-permute-start(f32[4,8,2048]{2,1,0:T(8,128)S(1)} %fusion.1), channel_id=1, source_target_pairs={{1,2},{3,4},{5,6},{7,8},{9,10},{11,12},{13,14},{2,1},{4,3},{6,5},{... | collective-permute-start | bytes 786440 | tf_op jit(solution)/shard_map/ppermute | solution.py:428
  5.5 4.0 %collective-permute-start.1 = (f32[16,2048]{1,0:T(8,128)S(1)}, f32[16,2048]{1,0:T(8,128)S(1)}, u32[]{:S(2)}, u32[]{:S(2)}) collective-permute-start(f32[16,2048]{1,0:T(8,128)S(1)} %copy-done.5), channel_id=1, source_target_pairs={{0,1},{1,0},{2,3},{3,2},{4,5},{5,4},{6,7},{7,6},{8,9},{9,8},{10,11... | collective-permute-start | bytes 393224 | tf_op jit(solution)/shard_map/ppermute | solution.py:423
  9.5 0.0 copy-done.6
  9.5 11.1 %all_to_all.10.links = s32[8,1,3]{2,1,0:T(1,128)S(1)} all-to-all(s32[8,1,3]{2,1,0:T(1,128)S(1)} %broadcast_in_dim.10.links), channel_id=1, replica_groups={{0,2,4,6,8,10,12,14},{1,3,5,7,9,11,13,15},{16,18,20,22,24,26,28,30},{17..., dimensions={0} | all-to-all | bytes 192 | tf_op jit(solution)/shard_map/all_to_all | solution.py:416
  20.7 0.0 collective-permute-done.pair.pair_state
  20.7 1.6 %strips.1 = f32[8,2,256]{2,1,0:T(2,128)} custom-call(s32[8,1,3]{2,1,0:T(1,128)S(1)} %all_to_all.10.links, f32[3,16,2048]{2,1,0:T(8,128)S(1)} %copy-done, f32[3,16,2048]{2,1,0:T(8,128)S(1)} %collective-permute-done.pair.pair_state), custom_call_target="tpu_custom_call" | custom-call | tf_op jit(solution)/shard_map/strips/pallas_call | solution.py:400
  22.3 0.0 collective-permute-done.2.edge
  22.3 3.3 %all-to-all-start.1 = ((f32[8,2,256]{2,1,0:T(2,128)}), f32[8,2,256]{2,1,0:T(2,128)S(1)}, u32[]{:S(2)}, u32[]{:S(2)}) async-start(f32[8,2,256]{2,1,0:T(2,128)} %strips.1), calls=%async_computation.1 | async-start | bytes 32768 | tf_op jit(solution)/shard_map/all_to_all | solution.py:432
  25.6 0.0 copy-start.2
  25.6 0.0 copy-start.4
  25.6 0.0 collective-permute-done.1.pair_depth
  25.6 3.2 %basin_steps.1 = f32[3,16,2048]{2,1,0:T(8,128)} custom-call(f32[3,16,2048]{2,1,0:T(8,128)S(1)} %copy-done, f32[16,2048]{1,0:T(8,128)S(1)} %copy-done.5, f32[3,16,2048]{2,1,0:T(8,128)S(1)} %collective-permute-done.pair.pair_state, f32[16,2048]{1,0:T(8,128)S(1)} %collective-permute-done.1.pair_depth, f32[4,8,2048]{2,1,0:T(8,128)S(1)} %collective-permute-done.2.edge), custom_call_target="tpu_custom_call" | custom-call | flops 8388608 | bytes 1441792 | tf_op jit(solution)/shard_map/basin_steps/pallas_call | solution.py:347
  28.9 3.3 %all-to-all-done.1.ghosts = f32[8,2,256]{2,1,0:T(2,128)S(1)} async-done(((f32[8,2,256]{2,1,0:T(2,128)}), f32[8,2,256]{2,1,0:T(2,128)S(1)}, u32[]{:S(2)}, u32[]{:S(2)}) %all-to-all-start.1) | async-done | bytes 16416 | tf_op jit(solution)/shard_map/all_to_all | solution.py:432
  32.1 0.0 copy-done.2
  32.1 0.0 copy-done.4
  32.1 9.5 %coast_steps.1 = f32[3,256,256]{2,1,0:T(8,128)} custom-call(s32[8,1,3]{2,1,0:T(1,128)S(1)} %broadcast_in_dim.10.links, f32[8,2,256]{2,1,0:T(2,128)S(1)} %all-to-all-done.1.ghosts, f32[3,2,32,8,128]{4,3,2,1,0:T(8,128)S(1)} %coast_fold.1.folded, f32[256,256]{1,0:T(8,128)S(1)} %bitcast.8, f32[2,256,256]{2,1,0:T(8,128)S(1)} %bitcast.6), custom_call_target="tpu_custom_call" | custom-call | flops 45875200 | bytes 1572864 | tf_op jit(solution)/shard_map/coast_steps/pallas_call | solution.py:274
  (2 shorter events, 0.0 us)
Async XLA Ops:
  0.6 1.0 %copy-start.1 = (f32[1,2,256,256]{3,2,1,0:T(8,128)S(1)}, f32[1,2,256,256]{3,2,1,0:T(8,128)}, u32[]{:S(2)}) copy-start(f32[1,2,256,256]{3,2,1,0:T(8,128)} %param.8) | copy-start | bytes 1572868
  1.7 0.9 %copy-start.3 = (f32[1,256,256]{2,1,0:T(8,128)S(1)}, f32[1,256,256]{2,1,0:T(8,128)}, u32[]{:S(2)}) copy-start(f32[1,256,256]{2,1,0:T(8,128)} %param.7) | copy-start | bytes 786436
  2.6 1.7 %copy-start = (f32[3,16,2048]{2,1,0:T(8,128)S(1)}, f32[3,16,2048]{2,1,0:T(8,128)}, u32[]{:S(2)}) copy-start(f32[3,16,2048]{2,1,0:T(8,128)} %state) | copy-start | bytes 1179652
  2.6 2.2 %copy-start.5 = (f32[16,2048]{1,0:T(8,128)S(1)}, f32[16,2048]{1,0:T(8,128)}, u32[]{:S(2)}) copy-start(f32[16,2048]{1,0:T(8,128)} %depth.1) | copy-start | bytes 393220
  4.3 16.4 %collective-permute-start = (f32[3,16,2048]{2,1,0:T(8,128)S(1)}, f32[3,16,2048]{2,1,0:T(8,128)S(1)}, u32[]{:S(2)}, u32[]{:S(2)}) collective-permute-start(f32[3,16,2048]{2,1,0:T(8,128)S(1)} %copy-done), channel_id=1, source_target_pairs={{0,1},{1,0},{2,3},{3,2},{4,5},{5,4},{6,7},{7,6},{8,9},{9,8},{10,11... | collective-permute-start | bytes 1179656 | tf_op jit(solution)/shard_map/ppermute | solution.py:423
  4.9 4.7 %copy-start.6 = (s32[1,3]{1,0:T(1,128)S(1)}, s32[1,3]{1,0:T(1,128)}, u32[]{:S(2)}) copy-start(s32[1,3]{1,0:T(1,128)} %param.9) | copy-start | bytes 40
  4.9 17.4 %collective-permute-start.2 = (f32[4,8,2048]{2,1,0:T(8,128)S(1)}, f32[4,8,2048]{2,1,0:T(8,128)S(1)}, u32[]{:S(2)}, u32[]{:S(2)}) collective-permute-start(f32[4,8,2048]{2,1,0:T(8,128)S(1)} %fusion.1), channel_id=1, source_target_pairs={{1,2},{3,4},{5,6},{7,8},{9,10},{11,12},{13,14},{2,1},{4,3},{6,5},{... | collective-permute-start | bytes 786440 | tf_op jit(solution)/shard_map/ppermute | solution.py:428
  5.5 20.1 %collective-permute-start.1 = (f32[16,2048]{1,0:T(8,128)S(1)}, f32[16,2048]{1,0:T(8,128)S(1)}, u32[]{:S(2)}, u32[]{:S(2)}) collective-permute-start(f32[16,2048]{1,0:T(8,128)S(1)} %copy-done.5), channel_id=1, source_target_pairs={{0,1},{1,0},{2,3},{3,2},{4,5},{5,4},{6,7},{7,6},{8,9},{9,8},{10,11... | collective-permute-start | bytes 393224 | tf_op jit(solution)/shard_map/ppermute | solution.py:423
  22.3 9.9 %all-to-all-start.1 = ((f32[8,2,256]{2,1,0:T(2,128)}), f32[8,2,256]{2,1,0:T(2,128)S(1)}, u32[]{:S(2)}, u32[]{:S(2)}) async-start(f32[8,2,256]{2,1,0:T(2,128)} %strips.1), calls=%async_computation.1 | async-start | bytes 32768 | tf_op jit(solution)/shard_map/all_to_all | solution.py:432
  25.6 6.5 %copy-start.2 = (f32[1,2,256,256]{3,2,1,0:T(8,128)S(1)}, f32[1,2,256,256]{3,2,1,0:T(8,128)}, u32[]{:S(2)}) copy-start(f32[1,2,256,256]{3,2,1,0:T(8,128)} %param.8) | copy-start | bytes 1572868
  25.6 6.5 %copy-start.4 = (f32[1,256,256]{2,1,0:T(8,128)S(1)}, f32[1,256,256]{2,1,0:T(8,128)}, u32[]{:S(2)}) copy-start(f32[1,256,256]{2,1,0:T(8,128)} %param.7) | copy-start | bytes 786436
where the time goes:
time: 41.9 us; the launch traced here: 41.6 us
  Pallas kernels  15.9 us (38%)
  blocking collectives  11.1 us (26%)
  starting transfers between devices  8.5 us (20%)
  waiting for transfers between devices  3.27 us (8%)
  local copies, waits for them, and re-layouts  2.02 us (5%)
  between operations  0.7 us (2%)
    all_to_all x1, blocking collectives, local(): lax.all_to_all(sent, 'row', 0, 0, axis_index_groups=parity, tiled=True)  11.1 us
    pallas_call x1, Pallas kernels, coast_run(): pl.pallas_call(coast_kernel, out_shape=jax.ShapeDtypeStruct((3, cells, ce...  9.47 us
    ppermute x2, starting transfers between devices, local(): lax.ppermute(a, 'row', twins)  4.48 us
    all_to_all x1, starting transfers between devices, local(): lax.all_to_all(ghosts, 'row', 0, 0, axis_index_groups=parity, tiled=True)  3.34 us
    all_to_all x1, waiting for transfers between devices, local(): lax.all_to_all(ghosts, 'row', 0, 0, axis_index_groups=parity, tiled=True)  3.26 us
    pallas_call x1, Pallas kernels, basin_run(): pl.pallas_call(basin_kernel, out_shape=jax.ShapeDtypeStruct((3, rows, wid...  3.22 us
    unnamed x14, local copies, waits for them, and re-layouts  2.01 us
    pallas_call x1, Pallas kernels, coast_fold(): pl.pallas_call(fold_kernel, out_shape=jax.ShapeDtypeStruct((3, 2, cells /...  1.66 us
  transfers between devices with their start and end apart: 4, of which 1 were waited for; matrix products, arithmetic and copies ran while one was open for 0% of the time, Pallas kernels for 12%

commit v1 on v0

--- a/solution.py
+++ b/solution.py
@@ -56,7 +56,7 @@
     ]
 
 
-def coast_steps(state, terms, after, parts, rows, group, steps, ghost):
+def coast_steps(state, terms, after, parts, opening, rows, group, steps, ghost):
     lane, sub = lane_ids(), row_ids()
     first, last = lane == 0, lane == LANES - 1
     top, bottom = sub == 0, sub == SUB - 1
@@ -110,11 +110,11 @@
         ]
 
     def step(_, carry):
-        tails, heads = [[cell_terms(u) for u in load(k)] for k in (rows - 1, 0)]
+        tails = [cell_terms(u) for u in load(rows - 1)]
         above = [wrapped(t, g) for t, g in zip(tails, ghost)]
-        start = [y_face(a, b) for a, b in zip(above, heads)]
-
-        def rows_from(begin, prev, acc):
+
+        def rows_from(trip, prev, acc):
+            begin = trip * group
             for k in range(group):
                 terms_of(begin, k)
             for k in range(group):
@@ -122,6 +122,10 @@
             for k in range(group):
                 cur = y_cells(begin, k)
                 face = [y_face(a, b) for a, b in zip(prev, cur)]
+                if k == 0:
+                    for half in range(2):
+                        for f in range(3):
+                            opening[trip, half, f] = face[half][f]
                 store(begin + k - 1, [[x + g for x, g in zip(*pair)] for pair in zip(acc, face)])
                 acc = [
                     [parts[k, f] - (parts[k, 6 + f] + face[0][f]) for f in range(3)],
@@ -133,15 +137,15 @@
         prev, acc = lax.fori_loop(
             0,
             rows // group,
-            lambda i, c: rows_from(i * group, *c),
+            lambda i, c: rows_from(i, *c),
             (above, [[zero] * 3 for _ in range(2)]),
         )
         end = [
             [
-                jnp.where(bottom, -(f + f), pltpu.roll(g, SUB - 1, 0))
-                for f, g in zip(cell["fy"], gs)
+                jnp.where(bottom, -(f + f), pltpu.roll(opening[0, half, i], SUB - 1, 0))
+                for i, f in enumerate(cell["fy"])
             ]
-            for cell, gs in zip(prev, start)
+            for half, cell in enumerate(prev)
         ]
         store(rows - 1, [[x + g for x, g in zip(*pair)] for pair in zip(acc, end)])
         return carry
@@ -220,15 +224,11 @@
     )(depth, flow)
 
 
-def coast_kernel(links, ghosts, folded, depth, flow, out, state, terms, after, parts, tmp):
+def coast_kernel(
+    links, ghosts, folded, depth, flow, out, state, terms, after, parts, opening, tmp, sems
+):
     rows = depth.shape[0] // SUB
     wet = links[0, 0, 2] > 0
-
-    def copy_dry(i, carry):
-        at = pl.ds(pl.multiple_of(i * TALL, TALL), TALL)
-        for f in range(3):
-            out[f, at] = depth[at] if f == 0 else flow[f - 1, at]
-        return carry
 
     def copy_in(k, carry):
         for f in range(3):
@@ -236,23 +236,16 @@
                 state[f, p, 1 + k] = folded[f, p, k]
         return carry
 
-    def unfold(k, carry):
-        for f in range(3):
-            both = join_columns(state[f, 0, 1 + k], state[f, 1, 1 + k])
-            for p in range(2):
-                tmp[f, p, pl.ds(k, SUB, stride=rows), :] = both[p]
-        return carry
-
-    def copy_out(i, carry):
-        at = pl.ds(pl.multiple_of(i * TALL, TALL), TALL)
-        for f in range(3):
-            for p in range(2):
-                out[f, at, HALVES[p]] = tmp[f, p, at] * (1.0 / UNITS[f])
-        return carry
-
     @pl.when(jnp.logical_not(wet))
     def _():
-        lax.fori_loop(0, depth.shape[0] // TALL, copy_dry, 0)
+        copies = [
+            pltpu.make_async_copy(depth, out.at[0], sems.at[0, 0]),
+            pltpu.make_async_copy(flow, out.at[1:], sems.at[0, 1]),
+        ]
+        for copy in copies:
+            copy.start()
+        for copy in copies:
+            copy.wait()
 
     @pl.when(wet)
     def _():
@@ -263,9 +256,24 @@
         spread = [jnp.broadcast_to(v[:, half], (SUB, LANES)) for v in (level, inflow) for half in HALVES]
         h, mv = split_columns(*spread[:2]), split_columns(*spread[2:])
         ghost = [cell_terms([h[p], jnp.zeros_like(h[p]), mv[p]]) for p in range(2)]
-        coast_steps(state, terms, after, parts, rows, GROUP, CSTEPS, ghost)
-        lax.fori_loop(0, rows, unfold, 0, unroll=4)
-        lax.fori_loop(0, depth.shape[0] // TALL, copy_out, 0)
+        coast_steps(state, terms, after, parts, opening, rows, GROUP, CSTEPS, ghost)
+        copies = []
+        for f in range(3):
+
+            def unfold(k, carry):
+                both = join_columns(state[f, 0, 1 + k], state[f, 1, 1 + k])
+                for p in range(2):
+                    tmp[f, p, pl.ds(k, SUB, stride=rows), :] = both[p] * (1.0 / UNITS[f])
+                return carry
+
+            lax.fori_loop(0, rows, unfold, 0, unroll=8)
+            for p in range(2):
+                copies.append(
+                    pltpu.make_async_copy(tmp.at[f, p], out.at[f, :, HALVES[p]], sems.at[f, p])
+                )
+                copies[-1].start()
+        for copy in copies:
+            copy.wait()
 
 
 def coast_run(links, ghosts, folded, depth, flow):
@@ -275,13 +283,15 @@
         coast_kernel,
         out_shape=jax.ShapeDtypeStruct((3, cells, cells), jnp.float32),
         in_specs=[pl.BlockSpec(memory_space=pltpu.SMEM), vmem, vmem, vmem, vmem],
-        out_specs=vmem,
+        out_specs=pl.BlockSpec(memory_space=pltpu.HBM),
         scratch_shapes=[
             pltpu.VMEM((3, 2, 1 + cells // SUB, SUB, LANES), jnp.float32),
             pltpu.VMEM((2, GROUP, 5, SUB, LANES), jnp.float32),
             pltpu.VMEM((GROUP, 6, SUB, LANES), jnp.float32),
             pltpu.VMEM((GROUP, 9, SUB, LANES), jnp.float32),
+            pltpu.VMEM((cells // SUB // GROUP, 2, 3, SUB, LANES), jnp.float32),
             pltpu.VMEM((3, 2, cells, LANES), jnp.float32),
+            pltpu.SemaphoreType.DMA((3, 2)),
         ],
         compiler_params=pltpu.CompilerParams(vmem_limit_bytes=VMEM_LIMIT),
         cost_estimate=pl.CostEstimate(
@@ -411,13 +421,13 @@
 def local(basin_state, basin_depth, coast_depth, coast_flow, coast_link):
     devices = lax.axis_size("row")
     odd = lax.axis_index("row") % 2
-    parity = [list(range(p, devices, 2)) for p in range(2)]
+    parity = [list(range(p, devices, 2))[::-1] for p in range(2)]
     sent = jnp.broadcast_to(coast_link, (devices // 2,) + coast_link.shape)
     links = lax.all_to_all(sent, "row", 0, 0, axis_index_groups=parity, tiled=True)
 
     depth, flow = coast_depth[0], coast_flow[0]
     folded = coast_fold(depth, flow)
-    basin_state, folded = lax.optimization_barrier((basin_state, folded))
+    links, basin_state, folded = lax.optimization_barrier((links, basin_state, folded))
 
     twins = [(i, i ^ 1) for i in range(devices)]
     pair_state, pair_depth = [lax.ppermute(a, "row", twins) for a in (basin_state, basin_depth)]

time: 41.9 us -> 43.9 us (1.048)
  starting transfers between devices: 8.5 us -> 23.3 us
  blocking collectives: 11.1 us -> 0 us
  waiting for transfers between devices: 3.27 us -> 0.01 us
  local copies, waits for them, and re-layouts: 2.02 us -> 3.24 us
    all_to_all x1 -> x0, blocking collectives: 11.1 us -> none  [local(): lax.all_to_all(sent, 'row', 0, 0, axis_index_groups=parity, tiled=True)]
    all_to_all x0 -> x1, starting transfers between devices: none -> 9.2 us  [local(): lax.all_to_all(sent, 'row', 0, 0, axis_index_groups=parity, tiled=True)]
    all_to_all x1, starting transfers between devices: 3.34 us -> 11.3 us  [local(): lax.all_to_all(ghosts, 'row', 0, 0, axis_index_groups=parity, tiled=True)]
    all_to_all x1, waiting for transfers between devices: 3.26 us -> 0.01 us  [local(): lax.all_to_all(ghosts, 'row', 0, 0, axis_index_groups=parity, tiled=True)]
    ppermute x2, starting transfers between devices: 4.48 us -> 2.04 us  [local(): lax.ppermute(a, 'row', twins)]
    unnamed x14, local copies, waits for them, and re-layouts: 2.01 us -> 2.65 us
    broadcast_in_dim x1, local copies, waits for them, and re-layouts: 0.01 us -> 0.59 us  [local(): sent = jnp.broadcast_to(coast_link, (devices // 2,) + coast_link.shape)]
  transfers between devices with their start and end apart: 4 -> 5, of which waited for: 1 -> 0; matrix products, arithmetic and copies ran while one was open for 0% -> 0% of each run, Pallas kernels for 12% -> 15%
where the time goes in v1:
time: 43.9 us; the launch traced here: 43.6 us
  starting transfers between devices  23.3 us (53%)
  Pallas kernels  16.3 us (37%)
  local copies, waits for them, and re-layouts  3.24 us (7%)
  between operations  0.71 us (2%)
    all_to_all x1, starting transfers between devices, local(): lax.all_to_all(ghosts, 'row', 0, 0, axis_index_groups=parity, tiled=True)  11.3 us
    pallas_call x1, Pallas kernels, coast_run(): pl.pallas_call(coast_kernel, out_shape=jax.ShapeDtypeStruct((3, cells, ce...  9.85 us
    all_to_all x1, starting transfers between devices, local(): lax.all_to_all(sent, 'row', 0, 0, axis_index_groups=parity, tiled=True)  9.2 us
    pallas_call x1, Pallas kernels, basin_run(): pl.pallas_call(basin_kernel, out_shape=jax.ShapeDtypeStruct((3, rows, wid...  3.22 us
    unnamed x14, local copies, waits for them, and re-layouts  2.65 us
    ppermute x2, starting transfers between devices, local(): lax.ppermute(a, 'row', twins)  2.04 us
    pallas_call x1, Pallas kernels, coast_fold(): pl.pallas_call(fold_kernel, out_shape=jax.ShapeDtypeStruct((3, 2, cells /...  1.66 us
    pallas_call x1, Pallas kernels, make_strips(): pl.pallas_call(strips_kernel, out_shape=jax.ShapeDtypeStruct((count, 2, c...  1.6 us
  transfers between devices with their start and end apart: 5, of which 0 were waited for; matrix products, arithmetic and copies ran while one was open for 0% of the time, Pallas kernels for 15%

profile of v1, /device:TPU:0, one launch (start us, length us, event | category | flops | bytes accessed | tf_op | source)
XLA Modules:
  0.0 43.6 jit_solution(9984394818486201202)
XLA Ops:
  0.6 0.0 copy-start.6
  0.6 0.6 %copy-done.6 = s32[1,3]{1,0:T(1,128)S(1)} copy-done((s32[1,3]{1,0:T(1,128)S(1)}, s32[1,3]{1,0:T(1,128)}, u32[]{:S(2)}) %copy-start.6) | copy-done | bytes 36
  1.3 0.6 %broadcast_in_dim.9.links = s32[8,1,3]{2,1,0:T(1,128)} broadcast(s32[3]{0:T(128)S(1)} %bitcast.11), dimensions={2} | broadcast | bytes 108 | tf_op jit(solution)/shard_map/broadcast_in_dim | solution.py:425
  1.9 9.2 %all-to-all-start = ((s32[8,1,3]{2,1,0:T(1,128)}), s32[8,1,3]{2,1,0:T(1,128)S(1)}, u32[]{:S(2)}, u32[]{:S(2)}) async-start(s32[8,1,3]{2,1,0:T(1,128)} %broadcast_in_dim.9.links), calls=%async_computation | async-start | bytes 8192 | tf_op jit(solution)/shard_map/all_to_all | solution.py:426
  11.1 0.0 copy-start.1
  11.1 1.0 %copy-done.1 = f32[1,2,256,256]{3,2,1,0:T(8,128)S(1)} copy-done((f32[1,2,256,256]{3,2,1,0:T(8,128)S(1)}, f32[1,2,256,256]{3,2,1,0:T(8,128)}, u32[]{:S(2)}) %copy-start.1) | copy-done | bytes 524312
  12.1 0.0 copy-start.3
  12.1 0.9 %copy-done.3 = f32[1,256,256]{2,1,0:T(8,128)S(1)} copy-done((f32[1,256,256]{2,1,0:T(8,128)S(1)}, f32[1,256,256]{2,1,0:T(8,128)}, u32[]{:S(2)}) %copy-start.3) | copy-done | bytes 262168
  13.1 0.0 copy-start
  13.1 0.0 copy-start.5
  13.1 1.7 %coast_fold.1.folded = f32[3,2,32,8,128]{4,3,2,1,0:T(8,128)S(1)} custom-call(f32[256,256]{1,0:T(8,128)S(1)} %bitcast.7, f32[2,256,256]{2,1,0:T(8,128)S(1)} %bitcast.5), custom_call_target="tpu_custom_call" | custom-call | flops 45875200 | bytes 1572864 | tf_op jit(solution)/shard_map/coast_fold/pallas_call | solution.py:213
  14.7 0.0 all-to-all-done.links
  14.8 0.0 copy-done
  14.8 0.1 collective-permute-start
  14.8 0.0 copy-done.5
  14.9 0.7 %collective-permute-start.2 = (f32[4,8,2048]{2,1,0:T(8,128)S(1)}, f32[4,8,2048]{2,1,0:T(8,128)S(1)}, u32[]{:S(2)}, u32[]{:S(2)}) collective-permute-start(f32[4,8,2048]{2,1,0:T(8,128)S(1)} %fusion.1), channel_id=1, source_target_pairs={{1,2},{3,4},{5,6},{7,8},{9,10},{11,12},{13,14},{2,1},{4,3},{6,5},{... | collective-permute-start | bytes 786440 | tf_op jit(solution)/shard_map/ppermute | solution.py:438
  15.6 2.0 %collective-permute-start.1 = (f32[16,2048]{1,0:T(8,128)S(1)}, f32[16,2048]{1,0:T(8,128)S(1)}, u32[]{:S(2)}, u32[]{:S(2)}) collective-permute-start(f32[16,2048]{1,0:T(8,128)S(1)} %copy-done.5), channel_id=1, source_target_pairs={{0,1},{1,0},{2,3},{3,2},{4,5},{5,4},{6,7},{7,6},{8,9},{9,8},{10,11... | collective-permute-start | bytes 393224 | tf_op jit(solution)/shard_map/ppermute | solution.py:433
  17.5 0.0 collective-permute-done.pair.pair_state
  17.6 1.6 %strips.1 = f32[8,2,256]{2,1,0:T(2,128)} custom-call(s32[8,1,3]{2,1,0:T(1,128)S(1)} %all-to-all-done.links, f32[3,16,2048]{2,1,0:T(8,128)S(1)} %copy-done, f32[3,16,2048]{2,1,0:T(8,128)S(1)} %collective-permute-done.pair.pair_state), custom_call_target="tpu_custom_call" | custom-call | tf_op jit(solution)/shard_map/strips/pallas_call | solution.py:410
  19.1 0.0 collective-permute-done.2.edge
  19.2 11.3 %all-to-all-start.1 = ((f32[8,2,256]{2,1,0:T(2,128)}), f32[8,2,256]{2,1,0:T(2,128)S(1)}, u32[]{:S(2)}, u32[]{:S(2)}) async-start(f32[8,2,256]{2,1,0:T(2,128)} %strips.1), calls=%async_computation.1 | async-start | bytes 32768 | tf_op jit(solution)/shard_map/all_to_all | solution.py:442
  30.5 0.0 copy-start.2
  30.5 0.0 copy-start.4
  30.5 0.0 collective-permute-done.1.pair_depth
  30.5 3.2 %basin_steps.1 = f32[3,16,2048]{2,1,0:T(8,128)} custom-call(f32[3,16,2048]{2,1,0:T(8,128)S(1)} %copy-done, f32[16,2048]{1,0:T(8,128)S(1)} %copy-done.5, f32[3,16,2048]{2,1,0:T(8,128)S(1)} %collective-permute-done.pair.pair_state, f32[16,2048]{1,0:T(8,128)S(1)} %collective-permute-done.1.pair_depth, f32[4,8,2048]{2,1,0:T(8,128)S(1)} %collective-permute-done.2.edge), custom_call_target="tpu_custom_call" | custom-call | flops 8388608 | bytes 1441792 | tf_op jit(solution)/shard_map/basin_steps/pallas_call | solution.py:357
  33.7 0.0 all-to-all-done.1.ghosts
  33.7 0.0 copy-done.2
  33.7 0.0 copy-done.4
  33.7 9.8 %coast_steps.1 = f32[3,256,256]{2,1,0:T(8,128)} custom-call(s32[8,1,3]{2,1,0:T(1,128)} %broadcast_in_dim.9.links, f32[8,2,256]{2,1,0:T(2,128)S(1)} %all-to-all-done.1.ghosts, f32[3,2,32,8,128]{4,3,2,1,0:T(8,128)S(1)} %coast_fold.1.folded, f32[256,256]{1,0:T(8,128)S(1)} %bitcast.8, f32[2,256,256]{2,1,0:T(8,128)S(1)} %bitcast.6), custom_call_target="tpu_custom_call" | custom-call | flops 45875200 | bytes 1572864 | tf_op jit(solution)/shard_map/coast_steps/pallas_call | solution.py:282
  (1 shorter events, 0.0 us)
Async XLA Ops:
  0.6 0.7 %copy-start.6 = (s32[1,3]{1,0:T(1,128)S(1)}, s32[1,3]{1,0:T(1,128)}, u32[]{:S(2)}) copy-start(s32[1,3]{1,0:T(1,128)} %param.9) | copy-start | bytes 40
  1.9 12.9 %all-to-all-start = ((s32[8,1,3]{2,1,0:T(1,128)}), s32[8,1,3]{2,1,0:T(1,128)S(1)}, u32[]{:S(2)}, u32[]{:S(2)}) async-start(s32[8,1,3]{2,1,0:T(1,128)} %broadcast_in_dim.9.links), calls=%async_computation | async-start | bytes 8192 | tf_op jit(solution)/shard_map/all_to_all | solution.py:426
  11.1 1.0 %copy-start.1 = (f32[1,2,256,256]{3,2,1,0:T(8,128)S(1)}, f32[1,2,256,256]{3,2,1,0:T(8,128)}, u32[]{:S(2)}) copy-start(f32[1,2,256,256]{3,2,1,0:T(8,128)} %param.8) | copy-start | bytes 1572868
  12.1 0.9 %copy-start.3 = (f32[1,256,256]{2,1,0:T(8,128)S(1)}, f32[1,256,256]{2,1,0:T(8,128)}, u32[]{:S(2)}) copy-start(f32[1,256,256]{2,1,0:T(8,128)} %param.7) | copy-start | bytes 786436
  13.1 1.7 %copy-start = (f32[3,16,2048]{2,1,0:T(8,128)S(1)}, f32[3,16,2048]{2,1,0:T(8,128)}, u32[]{:S(2)}) copy-start(f32[3,16,2048]{2,1,0:T(8,128)} %state) | copy-start | bytes 1179652
  13.1 1.8 %copy-start.5 = (f32[16,2048]{1,0:T(8,128)S(1)}, f32[16,2048]{1,0:T(8,128)}, u32[]{:S(2)}) copy-start(f32[16,2048]{1,0:T(8,128)} %depth.1) | copy-start | bytes 393220
  14.8 2.8 %collective-permute-start = (f32[3,16,2048]{2,1,0:T(8,128)S(1)}, f32[3,16,2048]{2,1,0:T(8,128)S(1)}, u32[]{:S(2)}, u32[]{:S(2)}) collective-permute-start(f32[3,16,2048]{2,1,0:T(8,128)S(1)} %copy-done), channel_id=1, source_target_pairs={{0,1},{1,0},{2,3},{3,2},{4,5},{5,4},{6,7},{7,6},{8,9},{9,8},{10,11... | collective-permute-start | bytes 1179656 | tf_op jit(solution)/shard_map/ppermute | solution.py:433
  14.9 4.3 %collective-permute-start.2 = (f32[4,8,2048]{2,1,0:T(8,128)S(1)}, f32[4,8,2048]{2,1,0:T(8,128)S(1)}, u32[]{:S(2)}, u32[]{:S(2)}) collective-permute-start(f32[4,8,2048]{2,1,0:T(8,128)S(1)} %fusion.1), channel_id=1, source_target_pairs={{1,2},{3,4},{5,6},{7,8},{9,10},{11,12},{13,14},{2,1},{4,3},{6,5},{... | collective-permute-start | bytes 786440 | tf_op jit(solution)/shard_map/ppermute | solution.py:438
  15.6 14.9 %collective-permute-start.1 = (f32[16,2048]{1,0:T(8,128)S(1)}, f32[16,2048]{1,0:T(8,128)S(1)}, u32[]{:S(2)}, u32[]{:S(2)}) collective-permute-start(f32[16,2048]{1,0:T(8,128)S(1)} %copy-done.5), channel_id=1, source_target_pairs={{0,1},{1,0},{2,3},{3,2},{4,5},{5,4},{6,7},{7,6},{8,9},{9,8},{10,11... | collective-permute-start | bytes 393224 | tf_op jit(solution)/shard_map/ppermute | solution.py:433
  19.2 14.6 %all-to-all-start.1 = ((f32[8,2,256]{2,1,0:T(2,128)}), f32[8,2,256]{2,1,0:T(2,128)S(1)}, u32[]{:S(2)}, u32[]{:S(2)}) async-start(f32[8,2,256]{2,1,0:T(2,128)} %strips.1), calls=%async_computation.1 | async-start | bytes 32768 | tf_op jit(solution)/shard_map/all_to_all | solution.py:442
  30.5 3.2 %copy-start.2 = (f32[1,2,256,256]{3,2,1,0:T(8,128)S(1)}, f32[1,2,256,256]{3,2,1,0:T(8,128)}, u32[]{:S(2)}) copy-start(f32[1,2,256,256]{3,2,1,0:T(8,128)} %param.8) | copy-start | bytes 1572868
  30.5 3.2 %copy-start.4 = (f32[1,256,256]{2,1,0:T(8,128)S(1)}, f32[1,256,256]{2,1,0:T(8,128)}, u32[]{:S(2)}) copy-start(f32[1,256,256]{2,1,0:T(8,128)} %param.7) | copy-start | bytes 786436

commit v2 on v0

--- a/solution.py
+++ b/solution.py
@@ -56,7 +56,7 @@
     ]
 
 
-def coast_steps(state, terms, after, parts, rows, group, steps, ghost):
+def coast_steps(state, terms, after, parts, opening, rows, group, steps, ghost):
     lane, sub = lane_ids(), row_ids()
     first, last = lane == 0, lane == LANES - 1
     top, bottom = sub == 0, sub == SUB - 1
@@ -110,11 +110,11 @@
         ]
 
     def step(_, carry):
-        tails, heads = [[cell_terms(u) for u in load(k)] for k in (rows - 1, 0)]
+        tails = [cell_terms(u) for u in load(rows - 1)]
         above = [wrapped(t, g) for t, g in zip(tails, ghost)]
-        start = [y_face(a, b) for a, b in zip(above, heads)]
-
-        def rows_from(begin, prev, acc):
+
+        def rows_from(trip, prev, acc):
+            begin = trip * group
             for k in range(group):
                 terms_of(begin, k)
             for k in range(group):
@@ -122,6 +122,10 @@
             for k in range(group):
                 cur = y_cells(begin, k)
                 face = [y_face(a, b) for a, b in zip(prev, cur)]
+                if k == 0:
+                    for half in range(2):
+                        for f in range(3):
+                            opening[trip, half, f] = face[half][f]
                 store(begin + k - 1, [[x + g for x, g in zip(*pair)] for pair in zip(acc, face)])
                 acc = [
                     [parts[k, f] - (parts[k, 6 + f] + face[0][f]) for f in range(3)],
@@ -133,15 +137,15 @@
         prev, acc = lax.fori_loop(
             0,
             rows // group,
-            lambda i, c: rows_from(i * group, *c),
+            lambda i, c: rows_from(i, *c),
             (above, [[zero] * 3 for _ in range(2)]),
         )
         end = [
             [
-                jnp.where(bottom, -(f + f), pltpu.roll(g, SUB - 1, 0))
-                for f, g in zip(cell["fy"], gs)
+                jnp.where(bottom, -(f + f), pltpu.roll(opening[0, half, i], SUB - 1, 0))
+                for i, f in enumerate(cell["fy"])
             ]
-            for cell, gs in zip(prev, start)
+            for half, cell in enumerate(prev)
         ]
         store(rows - 1, [[x + g for x, g in zip(*pair)] for pair in zip(acc, end)])
         return carry
@@ -220,7 +224,9 @@
     )(depth, flow)
 
 
-def coast_kernel(links, ghosts, folded, depth, flow, out, state, terms, after, parts, tmp):
+def coast_kernel(
+    links, ghosts, folded, depth, flow, out, state, terms, after, parts, opening, tmp
+):
     rows = depth.shape[0] // SUB
     wet = links[0, 0, 2] > 0
 
@@ -263,7 +269,7 @@
         spread = [jnp.broadcast_to(v[:, half], (SUB, LANES)) for v in (level, inflow) for half in HALVES]
         h, mv = split_columns(*spread[:2]), split_columns(*spread[2:])
         ghost = [cell_terms([h[p], jnp.zeros_like(h[p]), mv[p]]) for p in range(2)]
-        coast_steps(state, terms, after, parts, rows, GROUP, CSTEPS, ghost)
+        coast_steps(state, terms, after, parts, opening, rows, GROUP, CSTEPS, ghost)
         lax.fori_loop(0, rows, unfold, 0, unroll=4)
         lax.fori_loop(0, depth.shape[0] // TALL, copy_out, 0)
 
@@ -281,6 +287,7 @@
             pltpu.VMEM((2, GROUP, 5, SUB, LANES), jnp.float32),
             pltpu.VMEM((GROUP, 6, SUB, LANES), jnp.float32),
             pltpu.VMEM((GROUP, 9, SUB, LANES), jnp.float32),
+            pltpu.VMEM((cells // SUB // GROUP, 2, 3, SUB, LANES), jnp.float32),
             pltpu.VMEM((3, 2, cells, LANES), jnp.float32),
         ],
         compiler_params=pltpu.CompilerParams(vmem_limit_bytes=VMEM_LIMIT),
@@ -358,6 +365,9 @@
     )(state, depth, pair_state, pair_depth, edge)
 
 
+PLACES = 32
+
+
 def strips_kernel(links, own, pair, ghosts, strips):
     rows, width = own.shape[1], own.shape[2]
     count, cells = ghosts.shape[0], ghosts.shape[2]
@@ -381,14 +391,20 @@
         return carry
 
     lax.fori_loop(0, count, piece, 0, unroll=8)
-    at = lax.broadcasted_iota(jnp.int32, (LANES, cells), 0)
-    cols = lax.broadcasted_iota(jnp.int32, (LANES, cells), 1)
+    at = lax.broadcasted_iota(jnp.int32, (PLACES, cells), 0)
+    cols = lax.broadcasted_iota(jnp.int32, (PLACES, cells), 1)
     base = cols // 16
     weight = ((cols % 16).astype(jnp.float32) + 0.5) / 16.0
     mix = jnp.where(at == base, 1.0 - weight, 0.0) + jnp.where(at == base + 1, weight, 0.0)
-    values = jnp.dot(
-        strips[...], mix, precision=lax.Precision.HIGHEST, preferred_element_type=jnp.float32
+    parts, rest = [], strips[:, :PLACES]
+    for _ in range(3):
+        parts.append(rest.astype(jnp.bfloat16))
+        rest = rest - parts[-1].astype(jnp.float32)
+    products = jnp.dot(
+        jnp.concatenate(parts, axis=0), mix.astype(jnp.bfloat16), preferred_element_type=jnp.float32
     )
+    size = 2 * count
+    values = products[:size] + (products[size : 2 * size] + products[2 * size :])
     for b in range(count):
         ghosts[b] = values[2 * b : 2 * b + 2]
 
@@ -411,13 +427,12 @@
 def local(basin_state, basin_depth, coast_depth, coast_flow, coast_link):
     devices = lax.axis_size("row")
     odd = lax.axis_index("row") % 2
-    parity = [list(range(p, devices, 2)) for p in range(2)]
+    parity = [list(range(p, devices, 2))[::-1] for p in range(2)]
     sent = jnp.broadcast_to(coast_link, (devices // 2,) + coast_link.shape)
     links = lax.all_to_all(sent, "row", 0, 0, axis_index_groups=parity, tiled=True)
 
     depth, flow = coast_depth[0], coast_flow[0]
     folded = coast_fold(depth, flow)
-    basin_state, folded = lax.optimization_barrier((basin_state, folded))
 
     twins = [(i, i ^ 1) for i in range(devices)]
     pair_state, pair_depth = [lax.ppermute(a, "row", twins) for a in (basin_state, basin_depth)]
@@ -427,8 +442,9 @@
     across = [(i, i + 1) for i in range(1, devices - 1, 2)]
     edge = lax.ppermute(edge, "row", across + [(j, i) for i, j in across])
 
+    pair_state, folded = lax.optimization_barrier((pair_state, folded))
     ghosts = make_strips(links, basin_state, pair_state, coast_depth.shape[2])
-    edge, ghosts = lax.optimization_barrier((edge, ghosts))
+    basin_depth, ghosts = lax.optimization_barrier((basin_depth, ghosts))
     ghosts = lax.all_to_all(ghosts, "row", 0, 0, axis_index_groups=parity, tiled=True)
     basin_out = basin_run(basin_state, basin_depth, pair_state, pair_depth, edge)
     folded, basin_out = lax.optimization_barrier((folded, basin_out))

time: 41.9 us -> 38.8 us (0.926)
  blocking collectives: 11.1 us -> 0 us
  starting transfers between devices: 8.5 us -> 19.4 us
  waiting for transfers between devices: 3.27 us -> 0.58 us
  local copies, waits for them, and re-layouts: 2.02 us -> 0.61 us
  other arithmetic: 0.03 us -> 1.13 us
    all_to_all x1 -> x0, blocking collectives: 11.1 us -> none  [local(): lax.all_to_all(sent, 'row', 0, 0, axis_index_groups=parity, tiled=True)]
    all_to_all x0 -> x1, starting transfers between devices: none -> 6.77 us  [local(): lax.all_to_all(sent, 'row', 0, 0, axis_index_groups=parity, tiled=True)]
    all_to_all x1, starting transfers between devices: 3.34 us -> 7.46 us  [local(): lax.all_to_all(ghosts, 'row', 0, 0, axis_index_groups=parity, tiled=True)]
    all_to_all x1, waiting for transfers between devices: 3.26 us -> 0.01 us  [local(): lax.all_to_all(ghosts, 'row', 0, 0, axis_index_groups=parity, tiled=True)]
    unnamed x14 -> x10, local copies, waits for them, and re-layouts: 2.01 us -> 0.02 us
    select_n x1, other arithmetic: 0.03 us -> 1.13 us  [local(): edge = jnp.where(odd == 1, whole[:, rows - HALO:], whole[:, :HALO])]
    broadcast_in_dim x1, local copies, waits for them, and re-layouts: 0.01 us -> 0.59 us  [local(): sent = jnp.broadcast_to(coast_link, (devices // 2,) + coast_link.shape)]
    all_to_all x0 -> x1, waiting for transfers between devices: none -> 0.57 us  [local(): lax.all_to_all(sent, 'row', 0, 0, axis_index_groups=parity, tiled=True)]
  transfers between devices with their start and end apart: 4 -> 5, of which waited for: 1 -> 1; matrix products, arithmetic and copies ran while one was open for 0% -> 4% of each run, Pallas kernels for 12% -> 17%
where the time goes in v2:
time: 38.8 us; the launch traced here: 38.5 us
  starting transfers between devices  19.4 us (50%)
  Pallas kernels  16 us (41%)
  other arithmetic  1.13 us (3%)
  between operations  0.7 us (2%)
  local copies, waits for them, and re-layouts  0.61 us (2%)
  waiting for transfers between devices  0.58 us (1%)
    pallas_call x1, Pallas kernels, coast_run(): pl.pallas_call(coast_kernel, out_shape=jax.ShapeDtypeStruct((3, cells, ce...  9.56 us
    all_to_all x1, starting transfers between devices, local(): lax.all_to_all(ghosts, 'row', 0, 0, axis_index_groups=parity, tiled=True)  7.46 us
    all_to_all x1, starting transfers between devices, local(): lax.all_to_all(sent, 'row', 0, 0, axis_index_groups=parity, tiled=True)  6.77 us
    ppermute x2, starting transfers between devices, local(): lax.ppermute(a, 'row', twins)  4.5 us
    pallas_call x1, Pallas kernels, basin_run(): pl.pallas_call(basin_kernel, out_shape=jax.ShapeDtypeStruct((3, rows, wid...  3.22 us
    pallas_call x1, Pallas kernels, coast_fold(): pl.pallas_call(fold_kernel, out_shape=jax.ShapeDtypeStruct((3, 2, cells /...  1.67 us
    pallas_call x1, Pallas kernels, make_strips(): pl.pallas_call(strips_kernel, out_shape=jax.ShapeDtypeStruct((count, 2, c...  1.58 us
    select_n x1, other arithmetic, local(): edge = jnp.where(odd == 1, whole[:, rows - HALO:], whole[:, :HALO])  1.13 us
  transfers between devices with their start and end apart: 5, of which 1 were waited for; matrix products, arithmetic and copies ran while one was open for 4% of the time, Pallas kernels for 17%

profile of v2, /device:TPU:0, one launch (start us, length us, event | category | flops | bytes accessed | tf_op | source)
XLA Modules:
  0.0 38.5 jit_solution(1067239941981481434)
XLA Ops:
  0.6 0.0 copy-start.1
  0.6 0.5 %collective-permute-start = (f32[3,16,2048]{2,1,0:T(8,128)}, f32[3,16,2048]{2,1,0:T(8,128)S(1)}, u32[]{:S(2)}, u32[]{:S(2)}) collective-permute-start(f32[3,16,2048]{2,1,0:T(8,128)} %state.1), channel_id=1, source_target_pairs={{0,1},{1,0},{2,3},{3,2},{4,5},{5,4},{6,7},{7,6},{8,9},{9,8},{10,11... | collective-permute-start | bytes 1179656 | tf_op jit(solution)/shard_map/ppermute | solution.py:438
  1.2 0.0 copy-start.2
  1.2 1.1 %fusion.1 = f32[4,8,2048]{2,1,0:T(8,128)S(1)} fusion(f32[3,16,2048]{2,1,0:T(8,128)} %state.1, f32[1,16,2048]{2,1,0:T(8,128)} %bitcast.9, pred[]{:T(512)S(6)} %eq.5), kind=kLoop, calls=%fused_computation.3 | loop fusion | flops 196608 | bytes 786433 | tf_op jit(solution)/shard_map/jit(_where)/select_n | solution.py:441
  2.3 0.0 copy-start.4
  2.3 0.7 %collective-permute-start.2 = (f32[4,8,2048]{2,1,0:T(8,128)S(1)}, f32[4,8,2048]{2,1,0:T(8,128)S(1)}, u32[]{:S(2)}, u32[]{:S(2)}) collective-permute-start(f32[4,8,2048]{2,1,0:T(8,128)S(1)} %fusion.1), channel_id=1, source_target_pairs={{1,2},{3,4},{5,6},{7,8},{9,10},{11,12},{13,14},{2,1},{4,3},{6,5},{... | collective-permute-start | bytes 786440 | tf_op jit(solution)/shard_map/ppermute | solution.py:443
  3.0 4.0 %collective-permute-start.1 = (f32[16,2048]{1,0:T(8,128)}, f32[16,2048]{1,0:T(8,128)S(1)}, u32[]{:S(2)}, u32[]{:S(2)}) collective-permute-start(f32[16,2048]{1,0:T(8,128)} %depth), channel_id=1, source_target_pairs={{0,1},{1,0},{2,3},{3,2},{4,5},{5,4},{6,7},{7,6},{8,9},{9,8},{10,11... | collective-permute-start | bytes 393224 | tf_op jit(solution)/shard_map/ppermute | solution.py:438
  7.0 0.0 copy-done.4
  7.0 0.6 %broadcast_in_dim.9.links = s32[8,1,3]{2,1,0:T(1,128)} broadcast(s32[3]{0:T(128)S(1)} %bitcast.11), dimensions={2} | broadcast | bytes 108 | tf_op jit(solution)/shard_map/broadcast_in_dim | solution.py:431
  7.6 6.8 %all-to-all-start = ((s32[8,1,3]{2,1,0:T(1,128)}), s32[8,1,3]{2,1,0:T(1,128)S(1)}, u32[]{:S(2)}, u32[]{:S(2)}) async-start(s32[8,1,3]{2,1,0:T(1,128)} %broadcast_in_dim.9.links), calls=%async_computation | async-start | bytes 8192 | tf_op jit(solution)/shard_map/all_to_all | solution.py:432
  14.3 0.0 copy-done.1
  14.3 0.0 copy-done.2
  14.3 0.0 copy-start
  14.4 1.7 %coast_fold.1.folded = f32[3,2,32,8,128]{4,3,2,1,0:T(8,128)S(1)} custom-call(f32[256,256]{1,0:T(8,128)S(1)} %bitcast.7, f32[2,256,256]{2,1,0:T(8,128)S(1)} %bitcast.5), custom_call_target="tpu_custom_call" | custom-call | flops 45875200 | bytes 1572864 | tf_op jit(solution)/shard_map/coast_fold/pallas_call | solution.py:213
  16.0 0.0 copy-start.3
  16.0 0.0 collective-permute-done.pair.pair_state
  16.0 0.6 %all-to-all-done.links = s32[8,1,3]{2,1,0:T(1,128)S(1)} async-done(((s32[8,1,3]{2,1,0:T(1,128)}), s32[8,1,3]{2,1,0:T(1,128)S(1)}, u32[]{:S(2)}, u32[]{:S(2)}) %all-to-all-start) | async-done | bytes 128 | tf_op jit(solution)/shard_map/all_to_all | solution.py:432
  16.6 0.0 copy-done
  16.6 1.6 %strips.1 = f32[8,2,256]{2,1,0:T(2,128)} custom-call(s32[8,1,3]{2,1,0:T(1,128)S(1)} %all-to-all-done.links, f32[3,16,2048]{2,1,0:T(8,128)S(1)} %copy-done, f32[3,16,2048]{2,1,0:T(8,128)S(1)} %collective-permute-done.pair.pair_state), custom_call_target="tpu_custom_call" | custom-call | tf_op jit(solution)/shard_map/strips/pallas_call | solution.py:416
  18.2 7.5 %all-to-all-start.1 = ((f32[8,2,256]{2,1,0:T(2,128)}), f32[8,2,256]{2,1,0:T(2,128)S(1)}, u32[]{:S(2)}, u32[]{:S(2)}) async-start(f32[8,2,256]{2,1,0:T(2,128)} %strips.1), calls=%async_computation.1 | async-start | bytes 32768 | tf_op jit(solution)/shard_map/all_to_all | solution.py:448
  25.7 0.0 collective-permute-done.1.pair_depth
  25.7 0.0 collective-permute-done.2.edge
  25.7 0.0 copy-done.3
  25.7 3.2 %basin_steps.1 = f32[3,16,2048]{2,1,0:T(8,128)} custom-call(f32[3,16,2048]{2,1,0:T(8,128)S(1)} %copy-done, f32[16,2048]{1,0:T(8,128)S(1)} %copy-done.3, f32[3,16,2048]{2,1,0:T(8,128)S(1)} %collective-permute-done.pair.pair_state, f32[16,2048]{1,0:T(8,128)S(1)} %collective-permute-done.1.pair_depth, f32[4,8,2048]{2,1,0:T(8,128)S(1)} %collective-permute-done.2.edge), custom_call_target="tpu_custom_call" | custom-call | flops 8388608 | bytes 1441792 | tf_op jit(solution)/shard_map/basin_steps/pallas_call | solution.py:354
  28.9 0.0 all-to-all-done.1.ghosts
  28.9 9.6 %coast_steps.1 = f32[3,256,256]{2,1,0:T(8,128)} custom-call(s32[8,1,3]{2,1,0:T(1,128)} %broadcast_in_dim.9.links, f32[8,2,256]{2,1,0:T(2,128)S(1)} %all-to-all-done.1.ghosts, f32[3,2,32,8,128]{4,3,2,1,0:T(8,128)S(1)} %coast_fold.1.folded, f32[256,256]{1,0:T(8,128)S(1)} %bitcast.8, f32[2,256,256]{2,1,0:T(8,128)S(1)} %bitcast.6), custom_call_target="tpu_custom_call" | custom-call | flops 45875200 | bytes 1572864 | tf_op jit(solution)/shard_map/coast_steps/pallas_call | solution.py:280
Async XLA Ops:
  0.6 13.7 %copy-start.1 = (f32[1,2,256,256]{3,2,1,0:T(8,128)S(1)}, f32[1,2,256,256]{3,2,1,0:T(8,128)}, u32[]{:S(2)}) copy-start(f32[1,2,256,256]{3,2,1,0:T(8,128)} %param.8) | copy-start | bytes 1572868
  0.6 15.4 %collective-permute-start = (f32[3,16,2048]{2,1,0:T(8,128)}, f32[3,16,2048]{2,1,0:T(8,128)S(1)}, u32[]{:S(2)}, u32[]{:S(2)}) collective-permute-start(f32[3,16,2048]{2,1,0:T(8,128)} %state.1), channel_id=1, source_target_pairs={{0,1},{1,0},{2,3},{3,2},{4,5},{5,4},{6,7},{7,6},{8,9},{9,8},{10,11... | collective-permute-start | bytes 1179656 | tf_op jit(solution)/shard_map/ppermute | solution.py:438
  1.2 13.2 %copy-start.2 = (f32[1,256,256]{2,1,0:T(8,128)S(1)}, f32[1,256,256]{2,1,0:T(8,128)}, u32[]{:S(2)}) copy-start(f32[1,256,256]{2,1,0:T(8,128)} %param.7) | copy-start | bytes 786436
  2.3 4.7 %copy-start.4 = (s32[1,3]{1,0:T(1,128)S(1)}, s32[1,3]{1,0:T(1,128)}, u32[]{:S(2)}) copy-start(s32[1,3]{1,0:T(1,128)} %param.9) | copy-start | bytes 40
  2.3 23.4 %collective-permute-start.2 = (f32[4,8,2048]{2,1,0:T(8,128)S(1)}, f32[4,8,2048]{2,1,0:T(8,128)S(1)}, u32[]{:S(2)}, u32[]{:S(2)}) collective-permute-start(f32[4,8,2048]{2,1,0:T(8,128)S(1)} %fusion.1), channel_id=1, source_target_pairs={{1,2},{3,4},{5,6},{7,8},{9,10},{11,12},{13,14},{2,1},{4,3},{6,5},{... | collective-permute-start | bytes 786440 | tf_op jit(solution)/shard_map/ppermute | solution.py:443
  3.0 22.7 %collective-permute-start.1 = (f32[16,2048]{1,0:T(8,128)}, f32[16,2048]{1,0:T(8,128)S(1)}, u32[]{:S(2)}, u32[]{:S(2)}) collective-permute-start(f32[16,2048]{1,0:T(8,128)} %depth), channel_id=1, source_target_pairs={{0,1},{1,0},{2,3},{3,2},{4,5},{5,4},{6,7},{7,6},{8,9},{9,8},{10,11... | collective-permute-start | bytes 393224 | tf_op jit(solution)/shard_map/ppermute | solution.py:438
  7.6 9.1 %all-to-all-start = ((s32[8,1,3]{2,1,0:T(1,128)}), s32[8,1,3]{2,1,0:T(1,128)S(1)}, u32[]{:S(2)}, u32[]{:S(2)}) async-start(s32[8,1,3]{2,1,0:T(1,128)} %broadcast_in_dim.9.links), calls=%async_computation | async-start | bytes 8192 | tf_op jit(solution)/shard_map/all_to_all | solution.py:432
  14.3 2.3 %copy-start = (f32[3,16,2048]{2,1,0:T(8,128)S(1)}, f32[3,16,2048]{2,1,0:T(8,128)}, u32[]{:S(2)}) copy-start(f32[3,16,2048]{2,1,0:T(8,128)} %state.1) | copy-start | bytes 1179652
  16.0 9.6 %copy-start.3 = (f32[16,2048]{1,0:T(8,128)S(1)}, f32[16,2048]{1,0:T(8,128)}, u32[]{:S(2)}) copy-start(f32[16,2048]{1,0:T(8,128)} %depth) | copy-start | bytes 393220
  18.2 10.7 %all-to-all-start.1 = ((f32[8,2,256]{2,1,0:T(2,128)}), f32[8,2,256]{2,1,0:T(2,128)S(1)}, u32[]{:S(2)}, u32[]{:S(2)}) async-start(f32[8,2,256]{2,1,0:T(2,128)} %strips.1), calls=%async_computation.1 | async-start | bytes 32768 | tf_op jit(solution)/shard_map/all_to_all | solution.py:448

commit v3 on v2

--- a/solution.py
+++ b/solution.py
@@ -266,8 +266,7 @@
         values = jnp.sum(ghosts[...], axis=0)
         level = (ghost_level + values[0:1]) * DEPTH_UNIT
         inflow = values[1:2] * FLOW_UNIT
-        spread = [jnp.broadcast_to(v[:, half], (SUB, LANES)) for v in (level, inflow) for half in HALVES]
-        h, mv = split_columns(*spread[:2]), split_columns(*spread[2:])
+        h, mv = [[jnp.broadcast_to(v[:, half], (SUB, LANES)) for half in HALVES] for v in (level, inflow)]
         ghost = [cell_terms([h[p], jnp.zeros_like(h[p]), mv[p]]) for p in range(2)]
         coast_steps(state, terms, after, parts, opening, rows, GROUP, CSTEPS, ghost)
         lax.fori_loop(0, rows, unfold, 0, unroll=4)
@@ -298,13 +297,15 @@
     )(links, ghosts, folded, depth, flow)
 
 
-def basin_kernel(state, depth, pair_state, pair_depth, edge, out, eta, hu, hv, dep):
+def basin_kernel(state, depth, pair_state, pair_depth, edges, out, eta, hu, hv, dep):
     rows, width = depth.shape
     total = rows + 2 * HALO
     chunks = width // LANES
     position = lax.axis_index("row")
     odd = position % 2
-    north_inside = (position < lax.axis_size("row") - 1).astype(jnp.float32)
+    end = lax.axis_size("row") - 1
+    north_inside = (position < end).astype(jnp.float32)
+    edge_inside = jnp.logical_and(position > 0, position < end).astype(jnp.float32)
     pair_from = pl.multiple_of(odd * (rows - HALO), HALO)
     pair_at = pl.multiple_of((1 - odd) * (HALO + rows), HALO)
     edge_at = pl.multiple_of(odd * (HALO + rows), HALO)
@@ -312,7 +313,7 @@
         own, pair = (depth, pair_depth) if field == 3 else (state.at[field], pair_state.at[field])
         ref[HALO : HALO + rows] = own[...] * unit
         ref[pl.ds(pair_at, HALO)] = pair[pl.ds(pair_from, HALO)] * unit
-        ref[pl.ds(edge_at, HALO)] = edge[field] * unit
+        ref[pl.ds(edge_at, HALO)] = edges[odd, field] * (unit * edge_inside)
     lane = lax.broadcasted_iota(jnp.int32, (total, LANES), 1)
     first, last = lane == 0, lane == LANES - 1
     row = lax.broadcasted_iota(jnp.int32, (total, LANES), 0)
@@ -347,7 +348,7 @@
     out[2] = hv[own] * 2.0
 
 
-def basin_run(state, depth, pair_state, pair_depth, edge):
+def basin_run(state, depth, pair_state, pair_depth, edges):
     rows, width = depth.shape
     total = rows + 2 * HALO
     vmem = pl.BlockSpec(memory_space=pltpu.VMEM)
@@ -362,15 +363,12 @@
             flops=BSTEPS * 16 * total * width, bytes_accessed=4 * 11 * rows * width, transcendentals=0
         ),
         name="basin_steps",
-    )(state, depth, pair_state, pair_depth, edge)
-
-
-PLACES = 32
+    )(state, depth, pair_state, pair_depth, edges)
 
 
 def strips_kernel(links, own, pair, ghosts, strips):
     rows, width = own.shape[1], own.shape[2]
-    count, cells = ghosts.shape[0], ghosts.shape[2]
+    count = ghosts.shape[0]
     span = 2 * LANES
     position = lax.axis_index("row")
     tops = (position * rows, (position + 1 - 2 * (position % 2)) * rows)
@@ -391,22 +389,15 @@
         return carry
 
     lax.fori_loop(0, count, piece, 0, unroll=8)
-    at = lax.broadcasted_iota(jnp.int32, (PLACES, cells), 0)
-    cols = lax.broadcasted_iota(jnp.int32, (PLACES, cells), 1)
-    base = cols // 16
-    weight = ((cols % 16).astype(jnp.float32) + 0.5) / 16.0
-    mix = jnp.where(at == base, 1.0 - weight, 0.0) + jnp.where(at == base + 1, weight, 0.0)
-    parts, rest = [], strips[:, :PLACES]
-    for _ in range(3):
-        parts.append(rest.astype(jnp.bfloat16))
-        rest = rest - parts[-1].astype(jnp.float32)
-    products = jnp.dot(
-        jnp.concatenate(parts, axis=0), mix.astype(jnp.bfloat16), preferred_element_type=jnp.float32
-    )
-    size = 2 * count
-    values = products[:size] + (products[size : 2 * size] + products[2 * size :])
-    for b in range(count):
-        ghosts[b] = values[2 * b : 2 * b + 2]
+    lane = lane_ids()
+    for b in range(0, count, SUB // 2):
+        values = strips[2 * b : 2 * b + SUB, :]
+        low, high = pick(values, lane // 8), pick(values, lane // 8 + 1)
+        for p in range(2):
+            weight = ((2 * lane + p) % 16).astype(jnp.float32) / 16.0 + 0.5 / 16.0
+            both = (1.0 - weight) * low + weight * high
+            for i in range(SUB // 2):
+                ghosts[b + i, :, p * LANES : (p + 1) * LANES] = both[2 * i : 2 * i + 2]
 
 
 def make_strips(links, own, pair, cells):
@@ -439,14 +430,14 @@
     rows = basin_depth.shape[0]
     whole = jnp.concatenate([basin_state, basin_depth[None]], axis=0)
     edge = jnp.where(odd == 1, whole[:, rows - HALO :], whole[:, :HALO])
-    across = [(i, i + 1) for i in range(1, devices - 1, 2)]
-    edge = lax.ppermute(edge, "row", across + [(j, i) for i, j in across])
+    across = [[i, (i + 1) % devices] for i in range(1, devices, 2)]
+    edges = lax.all_gather(edge, "row", axis_index_groups=across)
 
     pair_state, folded = lax.optimization_barrier((pair_state, folded))
     ghosts = make_strips(links, basin_state, pair_state, coast_depth.shape[2])
     basin_depth, ghosts = lax.optimization_barrier((basin_depth, ghosts))
     ghosts = lax.all_to_all(ghosts, "row", 0, 0, axis_index_groups=parity, tiled=True)
-    basin_out = basin_run(basin_state, basin_depth, pair_state, pair_depth, edge)
+    basin_out = basin_run(basin_state, basin_depth, pair_state, pair_depth, edges)
     folded, basin_out = lax.optimization_barrier((folded, basin_out))
     coast_out = coast_run(sent, ghosts, folded, depth, flow)
     return (basin_out, coast_out[None])

time: 38.8 us -> 44.4 us (1.14)
  the two profiles are of different devices: /device:TPU:0 before, /device:TPU:1 now
where the time goes in v3:
time: 44.4 us; the launch traced here: 43.8 us
  Pallas kernels  15.8 us (36%)
  starting transfers between devices  14.8 us (33%)
  blocking collectives  9.33 us (21%)
  local copies, waits for them, and re-layouts  3.12 us (7%)
  between operations  0.69 us (2%)
    pallas_call x1, Pallas kernels, coast_run(): pl.pallas_call(coast_kernel, out_shape=jax.ShapeDtypeStruct((3, cells, ce...  9.42 us
    all_gather x1, blocking collectives, local(): edges = lax.all_gather(edge, 'row', axis_index_groups=across)  9.33 us
    all_to_all x1, starting transfers between devices, local(): lax.all_to_all(sent, 'row', 0, 0, axis_index_groups=parity, tiled=True)  8.42 us
    all_to_all x1, starting transfers between devices, local(): lax.all_to_all(ghosts, 'row', 0, 0, axis_index_groups=parity, tiled=True)  5.44 us
    pallas_call x1, Pallas kernels, basin_run(): pl.pallas_call(basin_kernel, out_shape=jax.ShapeDtypeStruct((3, rows, wid...  3.21 us
    unnamed x14, local copies, waits for them, and re-layouts  2.53 us
    pallas_call x1, Pallas kernels, coast_fold(): pl.pallas_call(fold_kernel, out_shape=jax.ShapeDtypeStruct((3, 2, cells /...  1.66 us
    pallas_call x1, Pallas kernels, make_strips(): pl.pallas_call(strips_kernel, out_shape=jax.ShapeDtypeStruct((count, 2, c...  1.52 us
  transfers between devices with their start and end apart: 4, of which 0 were waited for; matrix products, arithmetic and copies ran while one was open for 1% of the time, Pallas kernels for 15%

profile of v3, /device:TPU:1, one launch (start us, length us, event | category | flops | bytes accessed | tf_op | source)
XLA Modules:
  0.0 43.8 jit_solution(14697511616760313587)
XLA Ops:
  0.6 0.0 copy-start.6
  0.6 0.1 collective-permute-start
  0.8 0.5 %copy-done.6 = s32[1,3]{1,0:T(1,128)S(1)} copy-done((s32[1,3]{1,0:T(1,128)S(1)}, s32[1,3]{1,0:T(1,128)}, u32[]{:S(2)}) %copy-start.6) | copy-done | bytes 36
  1.3 0.6 %broadcast_in_dim.9.links = s32[8,1,3]{2,1,0:T(1,128)} broadcast(s32[3]{0:T(128)S(1)} %bitcast.13), dimensions={2} | broadcast | bytes 108 | tf_op jit(solution)/shard_map/broadcast_in_dim | solution.py:422
  1.9 8.4 %all-to-all-start = ((s32[8,1,3]{2,1,0:T(1,128)}), s32[8,1,3]{2,1,0:T(1,128)S(1)}, u32[]{:S(2)}, u32[]{:S(2)}) async-start(s32[8,1,3]{2,1,0:T(1,128)} %broadcast_in_dim.9.links), calls=%async_computation | async-start | bytes 8192 | tf_op jit(solution)/shard_map/all_to_all | solution.py:423
  10.3 0.9 %collective-permute-start.1 = (f32[16,2048]{1,0:T(8,128)}, f32[16,2048]{1,0:T(8,128)S(1)}, u32[]{:S(2)}, u32[]{:S(2)}) collective-permute-start(f32[16,2048]{1,0:T(8,128)} %depth), channel_id=1, source_target_pairs={{0,1},{1,0},{2,3},{3,2},{4,5},{5,4},{6,7},{7,6},{8,9},{9,8},{10,11... | collective-permute-start | bytes 393224 | tf_op jit(solution)/shard_map/ppermute | solution.py:429
  11.2 0.0 copy-start.1
  11.2 1.0 %copy-done.1 = f32[1,2,256,256]{3,2,1,0:T(8,128)S(1)} copy-done((f32[1,2,256,256]{3,2,1,0:T(8,128)S(1)}, f32[1,2,256,256]{3,2,1,0:T(8,128)}, u32[]{:S(2)}) %copy-start.1) | copy-done | bytes 524312
  12.2 0.0 copy-start.3
  12.2 0.9 %copy-done.3 = f32[1,256,256]{2,1,0:T(8,128)S(1)} copy-done((f32[1,256,256]{2,1,0:T(8,128)S(1)}, f32[1,256,256]{2,1,0:T(8,128)}, u32[]{:S(2)}) %copy-start.3) | copy-done | bytes 262168
  13.1 0.0 copy-start
  13.1 0.0 copy-start.5
  13.1 1.7 %coast_fold.1.folded = f32[3,2,32,8,128]{4,3,2,1,0:T(8,128)S(1)} custom-call(f32[256,256]{1,0:T(8,128)S(1)} %bitcast.9, f32[2,256,256]{2,1,0:T(8,128)S(1)} %bitcast.6), custom_call_target="tpu_custom_call" | custom-call | flops 45875200 | bytes 1572864 | tf_op jit(solution)/shard_map/coast_fold/pallas_call | solution.py:213
  14.8 0.0 copy-done
  14.8 0.0 copy-done.5
  14.9 0.0 collective-permute-done.pair.pair_state
  14.9 0.0 all-to-all-done.links
  14.9 1.5 %strips.1 = f32[8,2,256]{2,1,0:T(2,128)} custom-call(s32[8,1,3]{2,1,0:T(1,128)S(1)} %all-to-all-done.links, f32[3,16,2048]{2,1,0:T(8,128)S(1)} %copy-done, f32[3,16,2048]{2,1,0:T(8,128)S(1)} %collective-permute-done.pair.pair_state), custom_call_target="tpu_custom_call" | custom-call | tf_op jit(solution)/shard_map/strips/pallas_call | solution.py:407
  16.4 5.4 %all-to-all-start.1 = ((f32[8,2,256]{2,1,0:T(2,128)}), f32[8,2,256]{2,1,0:T(2,128)S(1)}, u32[]{:S(2)}, u32[]{:S(2)}) async-start(f32[8,2,256]{2,1,0:T(2,128)} %strips.1), calls=%async_computation.1 | async-start | bytes 32768 | tf_op jit(solution)/shard_map/all_to_all | solution.py:439
  21.8 9.3 %all-gather = f32[8,8,2048]{2,1,0:T(8,128)S(1)} all-gather(f32[4,8,2048]{2,1,0:T(8,128)S(1)} %fusion.1), channel_id=2, replica_groups={{1,2},{3,4},{5,6},{7,8},{9,10},{11,12},{13,14},{15,0},{17,18},{19,20},{..., dimensions={0}, use_global_device_ids=true | all-gather | bytes 786432 | tf_op jit(solution)/shard_map/all_gather | solution.py:434
  31.2 0.0 collective-permute-done.1.pair_depth
  31.2 0.0 copy-start.2
  31.2 0.0 copy-start.4
  31.2 3.2 %basin_steps.1 = f32[3,16,2048]{2,1,0:T(8,128)} custom-call(f32[3,16,2048]{2,1,0:T(8,128)S(1)} %copy-done, f32[16,2048]{1,0:T(8,128)S(1)} %copy-done.5, f32[3,16,2048]{2,1,0:T(8,128)S(1)} %collective-permute-done.pair.pair_state, f32[16,2048]{1,0:T(8,128)S(1)} %collective-permute-done.1.pair_depth, f32[2,4,8,2048]{3,2,1,0:T(8,128)S(1)} %bitcast.8), custom_call_target="tpu_custom_call" | custom-call | flops 8388608 | bytes 1441792 | tf_op jit(solution)/shard_map/basin_steps/pallas_call | solution.py:355
  34.4 0.0 all-to-all-done.1.ghosts
  34.4 0.0 copy-done.2
  34.4 0.0 copy-done.4
  34.4 9.4 %coast_steps.1 = f32[3,256,256]{2,1,0:T(8,128)} custom-call(s32[8,1,3]{2,1,0:T(1,128)} %broadcast_in_dim.9.links, f32[8,2,256]{2,1,0:T(2,128)S(1)} %all-to-all-done.1.ghosts, f32[3,2,32,8,128]{4,3,2,1,0:T(8,128)S(1)} %coast_fold.1.folded, f32[256,256]{1,0:T(8,128)S(1)} %bitcast.10, f32[2,256,256]{2,1,0:T(8,128)S(1)} %bitcast.7), custom_call_target="tpu_custom_call" | custom-call | flops 45875200 | bytes 1572864 | tf_op jit(solution)/shard_map/coast_steps/pallas_call | solution.py:279
  (1 shorter events, 0.0 us)
Async XLA Ops:
  0.6 0.7 %copy-start.6 = (s32[1,3]{1,0:T(1,128)S(1)}, s32[1,3]{1,0:T(1,128)}, u32[]{:S(2)}) copy-start(s32[1,3]{1,0:T(1,128)} %param.9) | copy-start | bytes 40
  0.6 14.2 %collective-permute-start = (f32[3,16,2048]{2,1,0:T(8,128)}, f32[3,16,2048]{2,1,0:T(8,128)S(1)}, u32[]{:S(2)}, u32[]{:S(2)}) collective-permute-start(f32[3,16,2048]{2,1,0:T(8,128)} %state.1), channel_id=1, source_target_pairs={{0,1},{1,0},{2,3},{3,2},{4,5},{5,4},{6,7},{7,6},{8,9},{9,8},{10,11... | collective-permute-start | bytes 1179656 | tf_op jit(solution)/shard_map/ppermute | solution.py:429
  1.9 13.0 %all-to-all-start = ((s32[8,1,3]{2,1,0:T(1,128)}), s32[8,1,3]{2,1,0:T(1,128)S(1)}, u32[]{:S(2)}, u32[]{:S(2)}) async-start(s32[8,1,3]{2,1,0:T(1,128)} %broadcast_in_dim.9.links), calls=%async_computation | async-start | bytes 8192 | tf_op jit(solution)/shard_map/all_to_all | solution.py:423
  10.3 20.9 %collective-permute-start.1 = (f32[16,2048]{1,0:T(8,128)}, f32[16,2048]{1,0:T(8,128)S(1)}, u32[]{:S(2)}, u32[]{:S(2)}) collective-permute-start(f32[16,2048]{1,0:T(8,128)} %depth), channel_id=1, source_target_pairs={{0,1},{1,0},{2,3},{3,2},{4,5},{5,4},{6,7},{7,6},{8,9},{9,8},{10,11... | collective-permute-start | bytes 393224 | tf_op jit(solution)/shard_map/ppermute | solution.py:429
  11.2 1.0 %copy-start.1 = (f32[1,2,256,256]{3,2,1,0:T(8,128)S(1)}, f32[1,2,256,256]{3,2,1,0:T(8,128)}, u32[]{:S(2)}) copy-start(f32[1,2,256,256]{3,2,1,0:T(8,128)} %param.8) | copy-start | bytes 1572868
  12.2 0.9 %copy-start.3 = (f32[1,256,256]{2,1,0:T(8,128)S(1)}, f32[1,256,256]{2,1,0:T(8,128)}, u32[]{:S(2)}) copy-start(f32[1,256,256]{2,1,0:T(8,128)} %param.7) | copy-start | bytes 786436
  13.1 1.7 %copy-start = (f32[3,16,2048]{2,1,0:T(8,128)S(1)}, f32[3,16,2048]{2,1,0:T(8,128)}, u32[]{:S(2)}) copy-start(f32[3,16,2048]{2,1,0:T(8,128)} %state.1) | copy-start | bytes 1179652
  13.1 1.7 %copy-start.5 = (f32[16,2048]{1,0:T(8,128)S(1)}, f32[16,2048]{1,0:T(8,128)}, u32[]{:S(2)}) copy-start(f32[16,2048]{1,0:T(8,128)} %depth) | copy-start | bytes 393220
  16.4 18.0 %all-to-all-start.1 = ((f32[8,2,256]{2,1,0:T(2,128)}), f32[8,2,256]{2,1,0:T(2,128)S(1)}, u32[]{:S(2)}, u32[]{:S(2)}) async-start(f32[8,2,256]{2,1,0:T(2,128)} %strips.1), calls=%async_computation.1 | async-start | bytes 32768 | tf_op jit(solution)/shard_map/all_to_all | solution.py:439
  31.2 3.2 %copy-start.2 = (f32[1,2,256,256]{3,2,1,0:T(8,128)S(1)}, f32[1,2,256,256]{3,2,1,0:T(8,128)}, u32[]{:S(2)}) copy-start(f32[1,2,256,256]{3,2,1,0:T(8,128)} %param.8) | copy-start | bytes 1572868
  31.2 3.2 %copy-start.4 = (f32[1,256,256]{2,1,0:T(8,128)S(1)}, f32[1,256,256]{2,1,0:T(8,128)}, u32[]{:S(2)}) copy-start(f32[1,256,256]{2,1,0:T(8,128)} %param.7) | copy-start | bytes 786436
